TPU v7x, 512 devices: a whole 4x8x8 slice. The times are simulated.
512 devices in a mesh: exp: 64 (over x, y, core), rep: 8 (over z).
Axes of the slice: x: 4, y: 8, z: 8, core: 2. Of those that a mesh axis runs over, the one named last changes fastest.
Arguments:
- passages_in: bfloat16 [92160, 2048], P(('exp', 'rep')), may hold values from -24 to 32
- routes: int32 [92160, 2], P(('exp', 'rep')), may hold values from 0 to 63, all different within a row; in each aligned block of 180 rows (0 to 179, 180 to 359, ...) at most 11 rows name the same one
- route_weights: float32 [92160, 2], P(('exp', 'rep')), may hold values from 0.2 to 1
- gate_weight: bfloat16 [64, 2048, 704], P('exp', 'rep'), may hold values from -0.125 to 0.125
- up_weight: bfloat16 [64, 2048, 704], P('exp', 'rep'), may hold values from -0.125 to 0.125
- down_weight: bfloat16 [64, 704, 2048], P('exp', None, 'rep'), may hold values from -0.21875 to 0.21875
- projection: bfloat16 [2048, 128], replicated, may hold values from -2 to 2
- queries: bfloat16 [128, 32, 128], P('rep'), may hold values from -6 to 6
- positives: int32 [128], replicated, may hold values from 0 to 511, as said below
Outputs:
- states: bfloat16 [92160, 2048], P(('exp', 'rep'))
- grad_projection: float32 [2048, 128], P('exp')
- mean_loss: float32 [], replicated
Inputs may be any that keep to these rules, and one draw needn't show every extreme that they name: `routes`: the two experts of a token differ. Among the rows of one device, no expert is named more than 11 times, and in some device's rows some expert is named exactly 11 times; every expert is named somewhere. `positives`: distinct queries have distinct positive passages.
All inputs are finite; a program needn't handle non-finite values.
Results may differ from a plain program's by a relative error of at most 0.0065.
Values may be sent and summed in bfloat16 or wider, within the bound.
No kernel may reach another device: no remote copies, remote signals or barrier semaphores. Data moves between devices by JAX's collectives and lax.ppermute only.
A program may use at most 64 MiB of HBM per device.

v0:
```python
import jax
import jax.numpy as jnp
from jax import lax
from jax.sharding import PartitionSpec as P

PAS_LEN = 180
soft_temp = 0.05
logit_gain = 1.5
norm_eps = 1e-06


def unit_rows(values):
    values = values.astype(jnp.float32)
    radius = jnp.sqrt(jnp.sum(values * values, axis=-1, keepdims=True) + norm_eps)
    return (values / radius, radius)


def token_scores(unit_block, query_rows, passage_count, query_count):
    scores = lax.dot_general(
        unit_block, query_rows, (((1,), (1,)), ((), ())), preferred_element_type=jnp.float32
    )
    weights = jnp.exp(scores / soft_temp)
    passage_len = unit_block.shape[0] // passage_count
    totals = jnp.sum(weights.reshape(passage_count, passage_len, -1), axis=1)
    logits = logit_gain * jnp.sum(
        (soft_temp * jnp.log(totals)).reshape(passage_count, query_count, -1), axis=2
    )
    return (weights, totals, logits)


def unit_grads(weights, totals, factor, query_rows, passage_count, query_count):
    passage_len = weights.shape[0] // passage_count
    query_len = weights.shape[1] // query_count
    shaped = weights.reshape(passage_count, passage_len, query_count, query_len) / totals.reshape(
        passage_count, 1, query_count, query_len
    )
    coeffs = (shaped * (logit_gain * factor)[:, None, :, None]).astype(jnp.bfloat16)
    coeffs = coeffs.reshape(passage_count * passage_len, query_count * query_len)
    return jnp.dot(coeffs, query_rows, preferred_element_type=jnp.float32)


def body(
    passages_in,
    routes,
    route_weights,
    gate_weight,
    up_weight,
    down_weight,
    projection,
    queries,
    positives,
):
    tok_count, model_width = passages_in.shape
    top_count = routes.shape[1]
    experts = lax.axis_size("exp")
    rep_count = lax.axis_size("rep")
    capacity = max(2, 2 * tok_count * top_count // experts)
    flat_route = routes.reshape(-1)
    onehot = (flat_route[:, None] == jnp.arange(experts, dtype=jnp.int32)[None, :]).astype(
        jnp.int32
    )
    slot_rank = jnp.sum((jnp.cumsum(onehot, axis=0) - onehot) * onehot, axis=1)
    places = flat_route * capacity + slot_rank
    sources = jnp.arange(tok_count * top_count, dtype=jnp.int32) // top_count
    outgoing = (
        jnp.zeros((experts * capacity, model_width), jnp.bfloat16)
        .at[places]
        .set(passages_in[sources])
    )
    arrived = lax.all_to_all(
        outgoing.reshape(experts, capacity, model_width),
        "exp",
        split_axis=0,
        concat_axis=0,
        tiled=True,
    )
    expert_rows = arrived.reshape(experts * capacity, model_width)

    def add_rows(shard_part):
        return jnp.dot(expert_rows, shard_part[0], preferred_element_type=jnp.float32)

    gate_sum = add_rows(lax.all_gather(gate_weight, "rep", axis=1, tiled=True))
    up_sum = add_rows(lax.all_gather(up_weight, "rep", axis=1, tiled=True))
    hidden = (jax.nn.silu(gate_sum) * up_sum).astype(jnp.bfloat16)
    expert_out = jnp.dot(
        hidden,
        lax.all_gather(down_weight, "rep", axis=2, tiled=True)[0],
        preferred_element_type=jnp.float32,
    ).astype(jnp.bfloat16)
    returned = lax.all_to_all(
        expert_out.reshape(experts, capacity, model_width),
        "exp",
        split_axis=0,
        concat_axis=0,
        tiled=True,
    )
    picked = returned.reshape(experts * capacity, model_width)[places].reshape(
        tok_count, top_count, model_width
    )
    mixed_sum = passages_in.astype(jnp.float32) + jnp.sum(
        route_weights[:, :, None] * picked.astype(jnp.float32), axis=1
    )
    states = mixed_sum.astype(jnp.bfloat16)
    projected = jnp.dot(states, projection, preferred_element_type=jnp.float32)
    unit_f32, radius = unit_rows(projected)
    unit_vec = unit_f32.astype(jnp.bfloat16)
    query_unit = unit_rows(queries)[0].astype(jnp.bfloat16)
    query_block, query_len, unit_width = queries.shape
    pas_count = tok_count // PAS_LEN
    total_queries = query_block * rep_count
    all_queries = lax.all_gather(query_unit, "rep", axis=0, tiled=True)
    query_rows = all_queries.reshape(total_queries * query_len, unit_width)
    owners = lax.axis_index(("exp", "rep")) * pas_count + jnp.arange(pas_count, dtype=jnp.int32)
    weights, totals, logits = token_scores(unit_vec, query_rows, pas_count, total_queries)
    positive_hit = owners[:, None] == positives[None, :]
    exp_logits = jnp.exp(logits)
    partition, pos_sum = lax.psum(
        (jnp.sum(exp_logits, axis=0), jnp.sum(jnp.where(positive_hit, logits, 0.0))), ("exp", "rep")
    )
    mean_loss = (jnp.sum(jnp.log(partition)) - pos_sum) / total_queries
    factor = exp_logits / partition[None, :] - positive_hit.astype(jnp.float32)
    grad_unit = unit_grads(weights, totals, factor, query_rows, pas_count, total_queries)
    grad_vec = (
        (grad_unit - unit_f32 * jnp.sum(unit_f32 * grad_unit, axis=1, keepdims=True)) / radius
    ).astype(jnp.bfloat16)
    row_sums = lax.psum_scatter(
        lax.dot_general(
            states, grad_vec, (((0,), (0,)), ((), ())), preferred_element_type=jnp.float32
        ),
        "exp",
        scatter_dimension=0,
        tiled=True,
    )
    grad_projection = lax.psum(row_sums, "rep")
    return (states, grad_projection, mean_loss)


def solution(mesh):
    in_specs = (
        P(("exp", "rep"), None),
        P(("exp", "rep"), None),
        P(("exp", "rep"), None),
        P("exp", "rep", None),
        P("exp", "rep", None),
        P("exp", None, "rep"),
        P(),
        P("rep", None, None),
        P(),
    )
    out_specs = (P(("exp", "rep"), None), P("exp", None), P())
    return jax.shard_map(body, mesh=mesh, in_specs=in_specs, out_specs=out_specs, check_vma=False)
```

profile of v0, /device:TPU:16, one launch (start us, length us, event | category | flops | bytes accessed | tf_op | source)
XLA Modules:
  0.0 605.3 jit_solution(8828364484753994428)
XLA Ops:
  8.7 0.8 copy.20
  9.7 0.9 reduce-window.6
  12.0 8.1 %scatter_custom_fusion = bf16[704,2048]{1,0:T(8,128)(2,1)S(1)} fusion(s32[360]{0:T(512)S(1)} %fusion.22, bf16[180,2048]{1,0:T(8,128)(2,1)} %param.9, s32[1024]{0:T(1024)S(1)} %pad_clamp_fusion.1, bf16[]{:T(256)} %constant.21.clone.1), kind=kCustom, calls=%fused_computation.16 | custom fusion | bytes 2884096 | tf_op jit(solution)/shard_map/scatter | solution.py:68
  20.1 2.9 reshape.185
  23.0 10.8 %all-to-all-start = ((bf16[64,11,2048]{2,1,0:T(8,128)(2,1)}), bf16[64,11,2048]{2,1,0:T(8,128)(2,1)}, u32[]{:S(2)}, u32[]{:S(2)}) async-start(bf16[64,11,2048]{2,1,0:T(8,128)(2,1)} %reshape.185), calls=%async_computation | async-start | bytes 8388608 | tf_op jit(solution)/shard_map/all_to_all | solution.py:70
  34.5 93.6 %all-to-all-done = bf16[64,11,2048]{2,1,0:T(8,128)(2,1)} async-done(((bf16[64,11,2048]{2,1,0:T(8,128)(2,1)}), bf16[64,11,2048]{2,1,0:T(8,128)(2,1)}, u32[]{:S(2)}, u32[]{:S(2)}) %all-to-all-start) | async-done | bytes 2883616 | tf_op jit(solution)/shard_map/all_to_all | solution.py:70
  128.1 3.4 reshape.186
  131.5 5.6 fusion.4
  137.1 44.8 %all-gather.9.cloned.1.call-done = bf16[1,704,2048]{2,1,0:T(8,128)(2,1)} async-done(((bf16[1,704,256]{2,1,0:T(8,128)(2,1)}), bf16[1,704,2048]{2,1,0:T(8,128)(2,1)}) %all-gather.9.cloned.1.call-update) | async-done | bytes 2883600 | tf_op jit(solution)/shard_map/all_gather | solution.py:87
  181.9 10.4 %convolution_convert_fusion = bf16[704,2048]{1,0:T(8,128)(2,1)} fusion(bf16[1,704,2048]{2,1,0:T(8,128)(2,1)} %all-gather.9.cloned.1.call-done, f32[704,704]{1,0:T(8,128)} %fusion.4, bf16[704,2048]{1,0:T(8,128)(2,1)S(1)} %reshape.186, bf16[1,2048,704]{1,2,0:T(8,128)(2,1)} %all-gather.7.cloned.1.call-done), kind=kOutput, calls=%fused_computation.5 | convolution fusion | flops 4064501760 | bytes 13516800 | tf_op jit(solution)/shard_map/dot_general | solution.py:85
  192.3 4.8 reshape.187
  197.1 10.5 %all-to-all-start.1 = ((bf16[64,11,2048]{2,1,0:T(8,128)(2,1)}), bf16[64,11,2048]{2,1,0:T(8,128)(2,1)}, u32[]{:S(2)}, u32[]{:S(2)}) async-start(bf16[64,11,2048]{2,1,0:T(8,128)(2,1)} %reshape.187), calls=%async_computation.1 | async-start | bytes 8388608 | tf_op jit(solution)/shard_map/all_to_all | solution.py:90
  207.8 0.8 fusion.15
  209.7 92.1 %all-to-all-done.1 = bf16[64,11,2048]{2,1,0:T(8,128)(2,1)} async-done(((bf16[64,11,2048]{2,1,0:T(8,128)(2,1)}), bf16[64,11,2048]{2,1,0:T(8,128)(2,1)}, u32[]{:S(2)}, u32[]{:S(2)}) %all-to-all-start.1) | async-done | bytes 2883616 | tf_op jit(solution)/shard_map/all_to_all | solution.py:90
  301.9 3.4 reshape.188
  305.3 3.1 gather_fusion
  308.4 3.4 reshape.191
  311.8 5.6 multiply_reduce_fusion
  318.0 3.8 fusion.28
  322.7 96.3 %all-reduce.1 = (f32[128]{0:T(128)S(1)}, f32[]{:T(128)}) all-reduce(f32[128]{0:T(128)S(1)} %get-tuple-element.8, f32[]{:T(128)} %get-tuple-element.7), channel_id=1, replica_groups=mesh['exp'=64,'rep'=8] {'exp','rep'}, use_global_device_ids=true, to_apply=%region_9.10 | all-reduce | flops 129 | bytes 1032 | tf_op jit(solution)/shard_map/psum | solution.py:117
  419.7 2.5 multiply_reduce_fusion.1
  422.2 1.6 fusion.18
  425.1 141.1 %reduce-scatter.2.cloned.1.call-done = f32[32,128]{1,0:T(8,128)} async-done(((f32[2048,128]{1,0:T(8,128)}), f32[32,128]{1,0:T(8,128)}) %reduce-scatter.2.cloned.1.call-update) | async-done | bytes 16400 | tf_op jit(solution)/shard_map/reduce_scatter | solution.py:126
  566.2 31.5 %psum.22 = f32[32,128]{1,0:T(8,128)} all-reduce(f32[32,128]{1,0:T(8,128)} %reduce-scatter.2.cloned.1.call-done), channel_id=1, replica_groups=mesh['exp'=64,'rep'=8] {'rep'}, use_global_device_ids=true, to_apply=%region_12.13 | all-reduce | flops 4096 | bytes 32768 | tf_op jit(solution)/shard_map/psum | solution.py:134
  (54 shorter events, 7.3 us)
Async XLA Ops:
  7.2 310.3 %copy-start = (bf16[2048,128]{1,0:T(8,128)(2,1)S(1)}, bf16[2048,128]{1,0:T(8,128)(2,1)}, u32[]{:S(2)}) copy-start(bf16[2048,128]{1,0:T(8,128)(2,1)} %param.15) | copy-start | bytes 1572868
  7.2 124.3 %all-gather.5.cloned.1.call-start = ((), (), s32[]{:S(2)}) async-start(), calls=%async_computation.3 | async-start | bytes 3244032 | tf_op jit(solution)/shard_map/all_gather | solution.py:82
  7.9 129.2 %all-gather.7.cloned.1.call-start = ((), (), s32[]{:S(2)}) async-start(), calls=%async_computation.4 | async-start | bytes 3244032 | tf_op jit(solution)/shard_map/all_gather | solution.py:83
  23.0 105.1 %all-to-all-start = ((bf16[64,11,2048]{2,1,0:T(8,128)(2,1)}), bf16[64,11,2048]{2,1,0:T(8,128)(2,1)}, u32[]{:S(2)}, u32[]{:S(2)}) async-start(bf16[64,11,2048]{2,1,0:T(8,128)(2,1)} %reshape.185), calls=%async_computation | async-start | bytes 8388608 | tf_op jit(solution)/shard_map/all_to_all | solution.py:70
  33.7 148.2 %all-gather.9.cloned.1.call-start = ((), (), s32[]{:S(2)}) async-start(), calls=%async_computation.5 | async-start | bytes 3244032 | tf_op jit(solution)/shard_map/all_gather | solution.py:87
  197.1 10.6 %copy-start.4 = (bf16[16,32,128]{2,1,0:T(8,128)(2,1)S(1)}, bf16[16,32,128]{2,1,0:T(8,128)(2,1)}, u32[]{:S(2)}) copy-start(bf16[16,32,128]{2,1,0:T(8,128)(2,1)} %param.16) | copy-start | bytes 393220
  197.1 11.9 %copy-start.5 = (f32[180,2]{0,1:T(2,128)S(1)}, f32[180,2]{0,1:T(2,128)}, u32[]{:S(2)}) copy-start(f32[180,2]{0,1:T(2,128)} %param.11) | copy-start | bytes 4324
  197.1 104.8 %all-to-all-start.1 = ((bf16[64,11,2048]{2,1,0:T(8,128)(2,1)}), bf16[64,11,2048]{2,1,0:T(8,128)(2,1)}, u32[]{:S(2)}, u32[]{:S(2)}) async-start(bf16[64,11,2048]{2,1,0:T(8,128)(2,1)} %reshape.187), calls=%async_computation.1 | async-start | bytes 8388608 | tf_op jit(solution)/shard_map/all_to_all | solution.py:90
  207.6 110.4 %all-gather.11.cloned.1.call-start = ((), (), s32[]{:S(2)}) async-start(), calls=%async_computation.6 | async-start | bytes 1179648 | tf_op jit(solution)/shard_map/all_gather | solution.py:111
  208.7 357.5 %reduce-scatter.2.cloned.1.call-start = ((), (), s32[]{:S(2)}) async-start(), calls=%async_computation.7 | async-start | bytes 1064960 | tf_op jit(solution)/shard_map/reduce_scatter | solution.py:126
  311.7 5.6 copy-start.3
  317.5 104.7 %copy-start.1 = (bf16[180,2048]{1,0:T(8,128)(2,1)}, bf16[180,2048]{1,0:T(8,128)(2,1)S(1)}, u32[]{:S(2)}) copy-start(bf16[180,2048]{1,0:T(8,128)(2,1)S(1)} %add_convert_fusion) | copy-start | bytes 2211844
  317.5 4.5 copy-start.6
  318.0 101.6 %copy-start.2 = (bf16[128,32,128]{2,1,0:T(8,128)(2,1)S(1)}, bf16[128,32,128]{2,1,0:T(8,128)(2,1)}, u32[]{:S(2)}) copy-start(bf16[128,32,128]{2,1,0:T(8,128)(2,1)} %all-gather.11.cloned.1.call-done) | copy-start | bytes 3145732
Sparse Core Ops, SparseCore 0:
  10.0 59.7 all-gather.4
  71.8 53.6 all-gather.6
  127.5 54.4 all-gather.8
  210.2 40.1 all-gather.10
  423.9 142.2 reduce-scatter.1
where the time goes:
time: 606 us; the launch traced here: 605 us
  waiting for transfers between devices  374 us (62%)
  blocking collectives  128 us (21%)
  local copies, waits for them, and re-layouts  31.4 us (5%)
  matrix products  24.3 us (4%)
  starting transfers between devices  21.9 us (4%)
  between operations  16.5 us (3%)
  other arithmetic  9.89 us (2%)
    reduce_scatter x1, waiting for transfers between devices, body(): lax.psum_scatter(lax.dot_general(states, grad_vec, (((0,), (0,)), ((), ()...  141 us
    psum x1, blocking collectives, body(): lax.psum((jnp.sum(exp_logits, axis=0), jnp.sum(jnp.where(positive_hit, lo...  96.3 us
    all_to_all x1, waiting for transfers between devices, body(): lax.all_to_all(outgoing.reshape(experts, capacity, model_width), 'exp', s...  93.6 us
    all_to_all x1, waiting for transfers between devices, body(): lax.all_to_all(expert_out.reshape(experts, capacity, model_width), 'exp',...  92.1 us
    all_gather x1, waiting for transfers between devices, body(): lax.all_gather(down_weight, 'rep', axis=2, tiled=True)[0]  44.8 us
    psum x1, blocking collectives, body(): grad_projection = lax.psum(row_sums, 'rep')  31.5 us
  transfers between devices with their start and end apart: 7, of which 4 were waited for; matrix products, arithmetic and copies ran while one was open for 7% of the time, Pallas kernels for 0%

commit v1 on v0

--- a/solution.py
+++ b/solution.py
@@ -2,6 +2,7 @@
 import jax.numpy as jnp
 from jax import lax
 from jax.sharding import PartitionSpec as P
+from jax.lax import all_to_all, psum
 
 PAS_LEN = 180
 soft_temp = 0.05
@@ -82,10 +83,18 @@
     gate_sum = add_rows(lax.all_gather(gate_weight, "rep", axis=1, tiled=True))
     up_sum = add_rows(lax.all_gather(up_weight, "rep", axis=1, tiled=True))
     hidden = (jax.nn.silu(gate_sum) * up_sum).astype(jnp.bfloat16)
+
+    def _attach_cubes(sheet):
+        w2 = jnp.concatenate(
+            all_to_all(
+                jnp.stack(tuple((sheet for _ in range(psum(1, "rep")))), axis=0), "rep", 0, 0
+            ),
+            axis=2,
+        )
+        return w2
+
     expert_out = jnp.dot(
-        hidden,
-        lax.all_gather(down_weight, "rep", axis=2, tiled=True)[0],
-        preferred_element_type=jnp.float32,
+        hidden, _attach_cubes(down_weight)[0], preferred_element_type=jnp.float32
     ).astype(jnp.bfloat16)
     returned = lax.all_to_all(
         expert_out.reshape(experts, capacity, model_width),

time: 606 us -> 640 us (1.056)
  waiting for transfers between devices: 374 us -> 394 us
  starting transfers between devices: 21.9 us -> 31.3 us
    all_to_all x0 -> x1, waiting for transfers between devices: none -> 68.1 us  [_attach_cubes(): all_to_all(jnp.stack(tuple((sheet for _ in range(psum(1, 'rep')))), axis=...]
    all_gather x1 -> x0, waiting for transfers between devices: 44.8 us -> none  [body(): lax.all_gather(down_weight, 'rep', axis=2, tiled=True)[0]]
    all_to_all x0 -> x1, starting transfers between devices: none -> 10.4 us  [_attach_cubes(): all_to_all(jnp.stack(tuple((sheet for _ in range(psum(1, 'rep')))), axis=...]
where the time goes in v1:
time: 640 us; the launch traced here: 639 us
  waiting for transfers between devices  394 us (62%)
  blocking collectives  126 us (20%)
  local copies, waits for them, and re-layouts  37.4 us (6%)
  starting transfers between devices  31.3 us (5%)
  matrix products  24.2 us (4%)
  between operations  16.5 us (3%)
  other arithmetic  9.2 us (1%)
    reduce_scatter x1, waiting for transfers between devices, body(): lax.psum_scatter(lax.dot_general(states, grad_vec, (((0,), (0,)), ((), ()...  143 us
    psum x1, blocking collectives, body(): lax.psum((jnp.sum(exp_logits, axis=0), jnp.sum(jnp.where(positive_hit, lo...  95.1 us
    all_to_all x1, waiting for transfers between devices, body(): lax.all_to_all(expert_out.reshape(experts, capacity, model_width), 'exp',...  92.1 us
    all_to_all x1, waiting for transfers between devices, body(): lax.all_to_all(outgoing.reshape(experts, capacity, model_width), 'exp', s...  89.7 us
    all_to_all x1, waiting for transfers between devices, _attach_cubes(): all_to_all(jnp.stack(tuple((sheet for _ in range(psum(1, 'rep')))), axis=...  68.1 us
    psum x1, blocking collectives, body(): grad_projection = lax.psum(row_sums, 'rep')  31.4 us
  transfers between devices with their start and end apart: 7, of which 4 were waited for; matrix products, arithmetic and copies ran while one was open for 7% of the time, Pallas kernels for 0%

profile of v1, /device:TPU:16, one launch (start us, length us, event | category | flops | bytes accessed | tf_op | source)
XLA Modules:
  0.0 639.1 jit_solution(17005552341865607009)
XLA Ops:
  7.2 2.8 stack.2
  10.0 10.4 %all-to-all-start.1 = ((bf16[8,1,704,256]{3,2,1,0:T(8,128)(2,1)}), bf16[8,1,704,256]{3,2,1,0:T(8,128)(2,1)}, u32[]{:S(2)}, u32[]{:S(2)}) async-start(bf16[8,1,704,256]{3,2,1,0:T(8,128)(2,1)} %stack.2), calls=%async_computation.1 | async-start | bytes 5767168 | tf_op jit(solution)/shard_map/all_to_all | solution.py:89
  23.2 8.2 %scatter_custom_fusion = bf16[704,2048]{1,0:T(8,128)(2,1)S(1)} fusion(s32[360]{0:T(512)S(1)} %fusion.21, bf16[180,2048]{1,0:T(8,128)(2,1)} %param.9, s32[1024]{0:T(1024)S(1)} %pad_clamp_fusion.1, bf16[]{:T(256)} %constant.21.clone.1), kind=kCustom, calls=%fused_computation.15 | custom fusion | bytes 2884096 | tf_op jit(solution)/shard_map/scatter | solution.py:69
  31.3 2.9 reshape.191
  34.2 68.1 %all-to-all-done.1 = bf16[8,1,704,256]{3,2,1,0:T(8,128)(2,1)} async-done(((bf16[8,1,704,256]{3,2,1,0:T(8,128)(2,1)}), bf16[8,1,704,256]{3,2,1,0:T(8,128)(2,1)}, u32[]{:S(2)}, u32[]{:S(2)}) %all-to-all-start.1) | async-done | bytes 2883616 | tf_op jit(solution)/shard_map/all_to_all | solution.py:89
  102.3 12.6 %all-to-all-start = ((bf16[64,11,2048]{2,1,0:T(8,128)(2,1)}), bf16[64,11,2048]{2,1,0:T(8,128)(2,1)}, u32[]{:S(2)}, u32[]{:S(2)}) async-start(bf16[64,11,2048]{2,1,0:T(8,128)(2,1)} %reshape.191), calls=%async_computation | async-start | bytes 8388608 | tf_op jit(solution)/shard_map/all_to_all | solution.py:71
  115.6 3.7 copy.26
  119.4 89.7 %all-to-all-done = bf16[64,11,2048]{2,1,0:T(8,128)(2,1)} async-done(((bf16[64,11,2048]{2,1,0:T(8,128)(2,1)}), bf16[64,11,2048]{2,1,0:T(8,128)(2,1)}, u32[]{:S(2)}, u32[]{:S(2)}) %all-to-all-start) | async-done | bytes 2883616 | tf_op jit(solution)/shard_map/all_to_all | solution.py:71
  209.1 3.4 reshape.192
  212.6 5.6 fusion.3
  218.2 10.3 %convolution_convert_fusion = bf16[704,2048]{1,0:T(8,128)(2,1)} fusion(bf16[704,2048]{1,0:T(8,128)(2,1)} %bitcast.39, f32[704,704]{1,0:T(8,128)} %fusion.3, bf16[704,2048]{1,0:T(8,128)(2,1)S(1)} %reshape.192, bf16[1,2048,704]{1,2,0:T(8,128)(2,1)} %all-gather.6.cloned.1.call-done), kind=kOutput, calls=%fused_computation.5 | convolution fusion | flops 4064501760 | bytes 13516800 | tf_op jit(solution)/shard_map/dot_general | solution.py:96
  228.5 4.8 reshape.194
  233.2 7.7 %all-to-all-start.2 = ((bf16[64,11,2048]{2,1,0:T(8,128)(2,1)}), bf16[64,11,2048]{2,1,0:T(8,128)(2,1)}, u32[]{:S(2)}, u32[]{:S(2)}) async-start(bf16[64,11,2048]{2,1,0:T(8,128)(2,1)} %reshape.194), calls=%async_computation.2 | async-start | bytes 8388608 | tf_op jit(solution)/shard_map/all_to_all | solution.py:99
  243.1 92.1 %all-to-all-done.2 = bf16[64,11,2048]{2,1,0:T(8,128)(2,1)} async-done(((bf16[64,11,2048]{2,1,0:T(8,128)(2,1)}), bf16[64,11,2048]{2,1,0:T(8,128)(2,1)}, u32[]{:S(2)}, u32[]{:S(2)}) %all-to-all-start.2) | async-done | bytes 2883616 | tf_op jit(solution)/shard_map/all_to_all | solution.py:99
  335.2 3.4 reshape.195
  338.6 3.1 gather_fusion
  341.7 3.4 reshape.198
  345.1 5.6 multiply_reduce_fusion
  351.4 3.8 fusion.27
  356.0 95.1 %all-reduce.1 = (f32[128]{0:T(128)S(1)}, f32[]{:T(128)}) all-reduce(f32[128]{0:T(128)S(1)} %get-tuple-element.8, f32[]{:T(128)} %get-tuple-element.7), channel_id=1, replica_groups=mesh['exp'=64,'rep'=8] {'exp','rep'}, use_global_device_ids=true, to_apply=%region_9.10 | all-reduce | flops 129 | bytes 1032 | tf_op jit(solution)/shard_map/psum | solution.py:126
  451.9 2.5 multiply_reduce_fusion.1
  454.4 1.6 fusion.17
  457.3 142.8 %reduce-scatter.2.cloned.1.call-done = f32[32,128]{1,0:T(8,128)} async-done(((f32[2048,128]{1,0:T(8,128)}), f32[32,128]{1,0:T(8,128)}) %reduce-scatter.2.cloned.1.call-update) | async-done | bytes 16400 | tf_op jit(solution)/shard_map/reduce_scatter | solution.py:135
  600.1 31.4 %psum.22 = f32[32,128]{1,0:T(8,128)} all-reduce(f32[32,128]{1,0:T(8,128)} %reduce-scatter.2.cloned.1.call-done), channel_id=1, replica_groups=mesh['exp'=64,'rep'=8] {'rep'}, use_global_device_ids=true, to_apply=%region_12.13 | all-reduce | flops 4096 | bytes 32768 | tf_op jit(solution)/shard_map/psum | solution.py:143
  (57 shorter events, 7.7 us)
Async XLA Ops:
  7.2 343.7 %copy-start = (bf16[2048,128]{1,0:T(8,128)(2,1)S(1)}, bf16[2048,128]{1,0:T(8,128)(2,1)}, u32[]{:S(2)}) copy-start(bf16[2048,128]{1,0:T(8,128)(2,1)} %param.15) | copy-start | bytes 1572868
  10.0 11.2 %copy-start.5 = (s32[180,2]{0,1:T(2,128)S(1)}, s32[180,2]{0,1:T(2,128)}, u32[]{:S(2)}) copy-start(s32[180,2]{0,1:T(2,128)} %param.10) | copy-start | bytes 4324
  10.0 92.3 %all-to-all-start.1 = ((bf16[8,1,704,256]{3,2,1,0:T(8,128)(2,1)}), bf16[8,1,704,256]{3,2,1,0:T(8,128)(2,1)}, u32[]{:S(2)}, u32[]{:S(2)}) async-start(bf16[8,1,704,256]{3,2,1,0:T(8,128)(2,1)} %stack.2), calls=%async_computation.1 | async-start | bytes 5767168 | tf_op jit(solution)/shard_map/all_to_all | solution.py:89
  20.5 192.1 %all-gather.4.cloned.1.call-start = ((), (), s32[]{:S(2)}) async-start(), calls=%async_computation.4 | async-start | bytes 3244032 | tf_op jit(solution)/shard_map/all_gather | solution.py:83
  102.3 106.8 %all-to-all-start = ((bf16[64,11,2048]{2,1,0:T(8,128)(2,1)}), bf16[64,11,2048]{2,1,0:T(8,128)(2,1)}, u32[]{:S(2)}, u32[]{:S(2)}) async-start(bf16[64,11,2048]{2,1,0:T(8,128)(2,1)} %reshape.191), calls=%async_computation | async-start | bytes 8388608 | tf_op jit(solution)/shard_map/all_to_all | solution.py:71
  114.9 103.3 %all-gather.6.cloned.1.call-start = ((), (), s32[]{:S(2)}) async-start(), calls=%async_computation.5 | async-start | bytes 3244032 | tf_op jit(solution)/shard_map/all_gather | solution.py:84
  233.2 7.8 %copy-start.4 = (bf16[16,32,128]{2,1,0:T(8,128)(2,1)S(1)}, bf16[16,32,128]{2,1,0:T(8,128)(2,1)}, u32[]{:S(2)}) copy-start(bf16[16,32,128]{2,1,0:T(8,128)(2,1)} %param.16) | copy-start | bytes 393220
  233.2 9.0 %copy-start.6 = (f32[180,2]{0,1:T(2,128)S(1)}, f32[180,2]{0,1:T(2,128)}, u32[]{:S(2)}) copy-start(f32[180,2]{0,1:T(2,128)} %param.11) | copy-start | bytes 4324
  233.2 102.0 %all-to-all-start.2 = ((bf16[64,11,2048]{2,1,0:T(8,128)(2,1)}), bf16[64,11,2048]{2,1,0:T(8,128)(2,1)}, u32[]{:S(2)}, u32[]{:S(2)}) async-start(bf16[64,11,2048]{2,1,0:T(8,128)(2,1)} %reshape.194), calls=%async_computation.2 | async-start | bytes 8388608 | tf_op jit(solution)/shard_map/all_to_all | solution.py:99
  241.0 110.4 %all-gather.8.cloned.1.call-start = ((), (), s32[]{:S(2)}) async-start(), calls=%async_computation.6 | async-start | bytes 1179648 | tf_op jit(solution)/shard_map/all_gather | solution.py:120
  242.0 358.1 %reduce-scatter.2.cloned.1.call-start = ((), (), s32[]{:S(2)}) async-start(), calls=%async_computation.7 | async-start | bytes 1064960 | tf_op jit(solution)/shard_map/reduce_scatter | solution.py:135
  345.1 5.6 copy-start.3
  350.9 103.6 %copy-start.1 = (bf16[180,2048]{1,0:T(8,128)(2,1)}, bf16[180,2048]{1,0:T(8,128)(2,1)S(1)}, u32[]{:S(2)}) copy-start(bf16[180,2048]{1,0:T(8,128)(2,1)S(1)} %add_convert_fusion) | copy-start | bytes 2211844
  350.9 4.5 copy-start.7
  351.4 100.5 %copy-start.2 = (bf16[128,32,128]{2,1,0:T(8,128)(2,1)S(1)}, bf16[128,32,128]{2,1,0:T(8,128)(2,1)}, u32[]{:S(2)}) copy-start(bf16[128,32,128]{2,1,0:T(8,128)(2,1)} %all-gather.8.cloned.1.call-done) | copy-start | bytes 3145732
Sparse Core Ops, SparseCore 0:
  23.3 97.3 all-gather.3
  122.7 51.7 all-gather.5
  243.9 39.0 all-gather.7
  456.1 143.9 reduce-scatter.1
